TPU v7x, 32 devices: a whole 2x2x4 slice. The times are simulated.
32 devices in a mesh: row: 8 (over z, core), col: 4 (over y, x).
Axes of the slice: x: 2, y: 2, z: 4, core: 2. Of those that a mesh axis runs over, the one named last changes fastest.
Arguments:
- static_design: bfloat16 [128, 2048], P('col', 'row'), may hold values from -6 to 6
- tv_design: bfloat16 [128, 12288], P('row', 'col'), may hold values from -0.5 to 0.5
- taps: float32 [32], replicated, may hold values from -1 to 1
- arc_id: int32 [128], replicated, may hold values from 0 to 3, never falling along the last dimension, each value on 1 to 64 neighbouring positions
Outputs:
- normal_block: float32 [2048, 12288], P('row', 'col')
Inputs may be any that keep to these rules, and one draw needn't show every extreme that they name: `arc_id`: arc numbers never fall along the rows; each arc has 1 to 64 rows and one has exactly 64.
All inputs are finite; a program needn't handle non-finite values.
Results may differ from a plain program's by a relative error of at most 0.0029.
Values may be sent and summed in bfloat16 or wider, within the bound.
A program may use at most 64 MiB of HBM per device.

v0:
```python
import jax
import jax.numpy as jnp
from jax import lax
from jax.sharding import PartitionSpec as P


def shift_down(values, steps, fill):
    pads = [(steps, 0)] + [(0, 0)] * (values.ndim - 1)
    return jnp.pad(values, pads, constant_values=fill)[: values.shape[0]]


def shift_up(values, steps, fill):
    pads = [(0, steps)] + [(0, 0)] * (values.ndim - 1)
    return jnp.pad(values, pads, constant_values=fill)[steps:]


def decorrelate(block, arcs, taps):
    count = taps.shape[0]
    forward = jnp.zeros(block.shape, jnp.float32)
    for step in range(count):
        same = (shift_down(arcs, step, -2) == arcs)[:, None]
        forward = forward + taps[step] * jnp.where(same, shift_down(block, step, 0.0), 0.0)
    backward = jnp.zeros(block.shape, jnp.float32)
    for step in range(count):
        same = (shift_up(arcs, step, -2) == arcs)[:, None]
        backward = backward + taps[step] * jnp.where(same, shift_up(forward, step, 0.0), 0.0)
    return backward


def body(static_design, tv_design, taps, arc_id):
    edge = taps.shape[0] - 1
    padded_arcs = jnp.pad(arc_id, (edge, edge), constant_values=-1)
    gathered = lax.all_gather(static_design, "col", axis=0, tiled=True)
    extended = jnp.pad(gathered.astype(jnp.float32), ((edge, edge), (0, 0)))
    whole_static = decorrelate(extended, padded_arcs, taps)[edge:-edge].astype(jnp.bfloat16)
    contract = (((0,), (0,)), ((), ()))
    all_rows = lax.all_gather(tv_design, "row", axis=0, tiled=True)
    return lax.dot_general(whole_static, all_rows, contract, preferred_element_type=jnp.float32)


def solution(mesh):
    return jax.shard_map(
        body,
        mesh=mesh,
        in_specs=(P("col", "row"), P("row", "col"), P(), P()),
        out_specs=P("row", "col"),
        check_vma=False,
    )
```

profile of v0, /device:TPU:0, one launch (start us, length us, event | category | flops | bytes accessed | tf_op | source)
XLA Modules:
  0.0 77.9 jit_solution(17534321659457541299)
XLA Ops:
  0.0 0.7 pad.509
  0.7 0.1 slice_compare_fusion.29
  0.8 1.8 %fusion.182 = (f32[1]{0:T(128)}, f32[1]{0:T(128)}, f32[1]{0:T(128)}, f32[1]{0:T(128)}, f32[1]{0:T(128)}, /*index=5*/f32[1]{0:T(128)}, f32[1]{0:T(128)}, f32[1]{0...) fusion(f32[32]{0:T(128)} %param.6), kind=kLoop, calls=%fused_computation.307 | loop fusion | bytes 104 | tf_op jit(solution)/shard_map/slice | solution.py:22
  2.6 0.1 slice_compare_fusion.30
  2.7 0.1 slice_compare_fusion.1
  2.8 0.1 slice.666
  2.9 0.1 slice_compare_fusion.2
  3.0 0.1 slice.664
  3.1 0.1 slice.668
  3.2 2.1 %fusion.181 = (f32[1]{0:T(128)}, f32[1]{0:T(128)}, f32[1]{0:T(128)}, f32[1]{0:T(128)}, f32[1]{0:T(128)}, /*index=5*/f32[1]{0:T(128)}, f32[1]{0:T(128)}, f32[1]{0...) fusion(f32[32]{0:T(128)} %param.6), kind=kLoop, calls=%fused_computation.306 | loop fusion | bytes 152 | tf_op jit(solution)/shard_map/slice | solution.py:26
  5.2 9.8 %all_gather.6 = bf16[128,256]{1,0:T(8,128)(2,1)S(1)} all-gather(bf16[32,256]{1,0:T(8,128)(2,1)} %param.4), channel_id=1, replica_groups=mesh['row'=8,'col'=4] {'col'}, dimensions={0}, use_global_device_ids=true | all-gather | bytes 81920 | tf_op jit(solution)/shard_map/all_gather | solution.py:33
  15.1 22.0 %fusion.128 = f32[190,256]{1,0:T(8,128)S(1)} fusion(f32[190,256]{1,0:T(8,128)S(1)} %pad_convert_fusion, f32[]{:T(128)} %bitcast.31, f32[]{:T(128)} %bitcast.30, f32[]{:T(128)} %bitcast.29, f32[]{:T(128)} %bitcast.28, f32[]{:T(128)} %bitcast.27, f32[]{:T(128)} %bitcast.26, f32[]{:T(128)} %bitcast.25, f32[]{:T(128)} %bitcast.24, f32[]{:T(128)} %bitcast.23, ...), kind=kLoop, calls=%fused_computation.186 | loop fusion | flops 4572160 | bytes 395138 | tf_op jit(solution)/shard_map/add | solution.py:22
  37.1 18.4 %fusion.146 = f32[190,256]{1,0:T(8,128)S(1)} fusion(f32[190,256]{1,0:T(8,128)S(1)} %fusion.128, f32[]{:T(128)} %bitcast.26, f32[]{:T(128)} %bitcast.25, f32[]{:T(128)} %bitcast.24, f32[]{:T(128)} %bitcast.23, f32[]{:T(128)} %bitcast.22, f32[]{:T(128)} %bitcast.21, f32[]{:T(128)} %bitcast.20, f32[]{:T(128)} %bitcast.19, f32[]{:T(128)} %bitcast.18, ...), kind=kLoop, calls=%fused_computation.204 | loop fusion | flops 3842560 | bytes 394168 | tf_op jit(solution)/shard_map/add | solution.py:26
  55.4 0.7 fusion.160
  56.2 16.7 %all_gather.7 = bf16[128,3072]{1,0:T(8,128)(2,1)S(1)} all-gather(bf16[16,3072]{1,0:T(8,128)(2,1)} %param.5), channel_id=1, replica_groups=mesh['row'=8,'col'=4] {'row'}, dimensions={0}, use_global_device_ids=true | all-gather | bytes 884736 | tf_op jit(solution)/shard_map/all_gather | solution.py:37
  72.9 5.0 %fusion.170 = f32[256,3072]{1,0:T(8,128)} fusion(bf16[128,3072]{1,0:T(8,128)(2,1)S(1)} %all_gather.7, f32[190,256]{1,0:T(8,128)S(1)} %get-tuple-element.7, f32[190,256]{1,0:T(8,128)S(1)} %get-tuple-element.6, f32[190,256]{1,0:T(8,128)S(1)} %get-tuple-element.8, f32[190,256]{1,0:T(8,128)S(1)} %get-tuple-element.9, f32[190,256]{1,0:T(8,128)S(1)} %get-tuple-element.5, ...), kind=kOutput, calls=%fused_computation.234 | convolution fusion | flops 201752576 | bytes 4720144 | tf_op jit(solution)/shard_map/dot_general | solution.py:38
  (1 shorter events, 0.0 us)
where the time goes:
time: 78.7 us; the launch traced here: 77.9 us
  other arithmetic  41.4 us (53%)
  blocking collectives  26.5 us (34%)
  matrix products  4.99 us (6%)
  local copies, waits for them, and re-layouts  4.84 us (6%)
    add x1, other arithmetic, decorrelate(): forward + taps[step] * jnp.where(same, shift_down(block, step, 0.0), 0.0)  22 us
    add x1, other arithmetic, decorrelate(): backward + taps[step] * jnp.where(same, shift_up(forward, step, 0.0), 0.0)  18.4 us
    all_gather x1, blocking collectives, body(): all_rows = lax.all_gather(tv_design, 'row', axis=0, tiled=True)  16.7 us
    all_gather x1, blocking collectives, body(): gathered = lax.all_gather(static_design, 'col', axis=0, tiled=True)  9.85 us
    dot_general x1, matrix products, body(): lax.dot_general(whole_static, all_rows, contract, preferred_element_type=...  4.99 us
    slice x1, local copies, waits for them, and re-layouts, decorrelate(): taps[step] * jnp.where(same, shift_up(forward, step, 0.0), 0.0)  2.06 us
    slice x1, local copies, waits for them, and re-layouts, decorrelate(): taps[step] * jnp.where(same, shift_down(block, step, 0.0), 0.0)  1.82 us

commit v1 on v0

v1 whole, which is shorter than its diff:
```python
import functools

import jax
import jax.numpy as jnp
from jax import lax
from jax.experimental import pallas as pl
from jax.experimental.pallas import tpu as pltpu
from jax.sharding import PartitionSpec as P

BLOCK = 128
MESH = pl.DeviceIdType.MESH
EXACT = lax.Precision.HIGHEST


def toeplitz(taps_ref, offset):
    shape = (BLOCK, BLOCK)
    lag = lax.broadcasted_iota(jnp.int32, shape, 0) - lax.broadcasted_iota(jnp.int32, shape, 1) + offset
    values = jnp.zeros(shape, jnp.float32)
    for step in range(taps_ref.shape[0]):
        values = jnp.where(lag == step, taps_ref[step], values)
    return values


def same_arc(rows, columns):
    shape = (BLOCK, BLOCK)
    down = jnp.transpose(jnp.broadcast_to(rows, shape))
    return down == jnp.broadcast_to(columns, shape)


def along(count, body, unrolled):
    if unrolled:
        for at in range(count):
            body(at)
    else:
        lax.fori_loop(0, count, lambda at, carry: (body(at), carry)[1], 0)


def kernel(
    n_row, n_col, pieces, taps_ref, arc_ref, static_ref, tv_ref, out_ref,
    static_all, tv_all, filter_ref, filtered_ref, weighted_ref,
    own_sem, static_send, static_recv, line_send, pair_send, tv_recv,
):
    row, col = lax.axis_index("row"), lax.axis_index("col")
    chips = n_row // 2
    chip, core = row // 2, row % 2
    static_rows, tv_rows = static_ref.shape[0], tv_ref.shape[0]
    width = tv_ref.shape[1] // pieces
    small = chips <= 4

    def at_row(chip_at, core_at):
        return (chip_at * 2 + core_at, col)

    has_up, has_down = chip < chips - 1, chip > 0

    barrier = pltpu.get_barrier_semaphore()
    for step in range(1, n_col):
        pl.semaphore_signal(barrier, inc=1, device_id=(row, (col + step) % n_col), device_id_type=MESH)
    pl.semaphore_signal(barrier, inc=1, device_id=at_row(chip, 1 - core), device_id_type=MESH)

    @pl.when(has_up)
    def _():
        pl.semaphore_signal(barrier, inc=1, device_id=at_row(chip + 1, core), device_id_type=MESH)

    @pl.when(has_down)
    def _():
        pl.semaphore_signal(barrier, inc=1, device_id=at_row(chip - 1, core), device_id_type=MESH)

    def static_rows_of(at):
        return static_all.at[pl.ds(pl.multiple_of(at * static_rows, static_rows), static_rows), :]

    def window(chip_at, core_at, piece):
        shard = chip_at * 2 + core_at
        rows = pl.ds(pl.multiple_of(shard * tv_rows, tv_rows), tv_rows)
        return tv_all.at[rows, pl.ds(piece * width, width)]

    def own_window(piece):
        return tv_ref.at[:, pl.ds(piece * width, width)]

    own_static = pltpu.make_async_copy(static_ref, static_rows_of(col), own_sem.at[0])
    own_tv = pltpu.make_async_copy(
        tv_ref, tv_all.at[pl.ds(pl.multiple_of(row * tv_rows, tv_rows), tv_rows), :], own_sem.at[1])
    own_static.start()
    own_tv.start()

    filter_ref[0] = toeplitz(taps_ref, 0)
    if arc_ref.shape[0] > 1:
        filter_ref[1] = toeplitz(taps_ref, BLOCK)

    pl.semaphore_wait(barrier, n_col + has_up.astype(jnp.int32) + has_down.astype(jnp.int32))

    def to_line(src, chip_at, piece, way):
        return pltpu.make_async_remote_copy(
            src_ref=src, dst_ref=window(chip_at, core, piece),
            send_sem=line_send.at[way, chip_at, piece], recv_sem=tv_recv.at[chip_at * 2 + core, piece],
            device_id=at_row(chip + 1 - 2 * way, core), device_id_type=MESH)

    def to_pair(src, chip_at, piece):
        return pltpu.make_async_remote_copy(
            src_ref=src, dst_ref=window(chip_at, core, piece),
            send_sem=pair_send.at[chip_at, piece], recv_sem=tv_recv.at[chip_at * 2 + core, piece],
            device_id=at_row(chip, 1 - core), device_id_type=MESH)

    def arrival(chip_at, core_at, piece):
        return pltpu.make_async_remote_copy(
            src_ref=window(chip_at, core_at, piece), dst_ref=window(chip_at, core_at, piece),
            send_sem=pair_send.at[chip_at, piece], recv_sem=tv_recv.at[chip_at * 2 + core_at, piece],
            device_id=at_row(chip, 1 - core), device_id_type=MESH)

    for piece in range(pieces):
        @pl.when(has_up)
        def _():
            to_line(own_window(piece), chip, piece, 0).start()

        @pl.when(has_down)
        def _():
            to_line(own_window(piece), chip, piece, 1).start()

    def to_col(step):
        peer = (col + step) % n_col
        return pltpu.make_async_remote_copy(
            src_ref=static_ref, dst_ref=static_rows_of(col),
            send_sem=static_send.at[step - 1], recv_sem=static_recv.at[step - 1],
            device_id=(row, peer), device_id_type=MESH)

    for step in range(1, n_col):
        to_col(step).start()
    for piece in range(pieces):
        to_pair(own_window(piece), chip, piece).start()

    def forward(hop, piece):
        below, above = chip - hop, chip + hop

        @pl.when(below >= 0)
        def _():
            arrival(below, core, piece).wait_recv()

            @pl.when(has_up)
            def _():
                to_line(window(below, core, piece), below, piece, 0).start()

            to_pair(window(below, core, piece), below, piece).start()

        @pl.when(above < chips)
        def _():
            arrival(above, core, piece).wait_recv()

            @pl.when(has_down)
            def _():
                to_line(window(above, core, piece), above, piece, 1).start()

            to_pair(window(above, core, piece), above, piece).start()

    def weigh():
        own_static.wait()
        for step in range(1, n_col):
            source = (col + n_col - step) % n_col
            pltpu.make_async_remote_copy(
                src_ref=static_ref, dst_ref=static_rows_of(source),
                send_sem=static_send.at[step - 1], recv_sem=static_recv.at[step - 1],
                device_id=(row, (col + step) % n_col), device_id_type=MESH).wait_recv()
        blocks = arc_ref.shape[0]
        contract = (((0,), (0,)), ((), ()))
        if blocks == 1:
            arcs = arc_ref[...]
            matrix = jnp.where(same_arc(arcs, arcs), filter_ref[0], 0.0)
            filtered = jnp.dot(matrix, static_all[...].astype(jnp.float32),
                               precision=EXACT, preferred_element_type=jnp.float32)
            weighted = lax.dot_general(filtered, matrix, contract,
                                       precision=EXACT, preferred_element_type=jnp.float32)
            weighted_ref[...] = weighted.astype(jnp.bfloat16)
            return

        def part(block, back):
            other = block - back
            inside = jnp.logical_and(other >= 0, block < blocks)
            here, there = jnp.minimum(block, blocks - 1), jnp.maximum(other, 0)
            arcs = same_arc(arc_ref[pl.ds(here, 1), :], arc_ref[pl.ds(there, 1), :])
            return jnp.where(jnp.logical_and(arcs, inside), filter_ref[back], 0.0)

        def rows_of(block):
            return pl.ds(pl.multiple_of(block * BLOCK, BLOCK), BLOCK)

        def first(block, carry):
            before = jnp.maximum(block - 1, 0)
            filtered_ref[rows_of(block), :] = jnp.dot(
                part(block, 0), static_all[rows_of(block), :].astype(jnp.float32),
                precision=EXACT, preferred_element_type=jnp.float32
            ) + jnp.dot(
                part(block, 1), static_all[rows_of(before), :].astype(jnp.float32),
                precision=EXACT, preferred_element_type=jnp.float32)
            return carry

        def second(block, carry):
            after = jnp.minimum(block + 1, blocks - 1)
            weighted = lax.dot_general(
                filtered_ref[rows_of(block), :], part(block, 0), contract,
                precision=EXACT, preferred_element_type=jnp.float32
            ) + lax.dot_general(
                filtered_ref[rows_of(after), :], part(block + 1, 1), contract,
                precision=EXACT, preferred_element_type=jnp.float32)
            weighted_ref[:, rows_of(block)] = weighted.astype(jnp.bfloat16)
            return carry

        lax.fori_loop(0, blocks, first, 0)
        lax.fori_loop(0, blocks, second, 0)

    def multiply(piece):
        def paired(chip_at):
            arrival(chip_at, 1 - core, piece).wait_recv()

        along(chips, paired, small)
        if piece == 0:
            own_tv.wait()
        columns = pl.ds(piece * width, width)
        out_ref[:, columns] = jnp.dot(
            weighted_ref[...], tv_all[:, columns], preferred_element_type=jnp.float32)

    for piece in range(pieces):
        forward(1, piece)
    weigh()

    def middle(at):
        for piece in range(pieces):
            forward(at + 2, piece)

    along(chips - 3, middle, small)
    for piece in range(pieces):
        forward(chips - 1, piece)
        if piece > 0:
            multiply(piece - 1)
    multiply(pieces - 1)

    for step in range(1, n_col):
        to_col(step).wait_send()

    def sent(chip_at):
        for piece in range(pieces):
            @pl.when(jnp.logical_and(has_up, chip_at <= chip))
            def _():
                to_line(own_window(piece), chip_at, piece, 0).wait_send()

            @pl.when(jnp.logical_and(has_down, chip_at >= chip))
            def _():
                to_line(own_window(piece), chip_at, piece, 1).wait_send()

            to_pair(own_window(piece), chip_at, piece).wait_send()

    along(chips, sent, small)


def body(static_design, tv_design, taps, arc_id, n_row, n_col):
    static_rows, static_width = static_design.shape
    tv_rows, tv_width = tv_design.shape
    rows = tv_rows * n_row
    pieces = 4 if n_row <= 8 else 1
    any_space = pl.BlockSpec(memory_space=pl.ANY)
    vmem = pl.BlockSpec(memory_space=pltpu.VMEM)
    return pl.pallas_call(
        functools.partial(kernel, n_row, n_col, pieces),
        out_shape=jax.ShapeDtypeStruct((static_width, tv_width), jnp.float32),
        in_specs=[pl.BlockSpec(memory_space=pltpu.SMEM), vmem, any_space, any_space],
        out_specs=vmem,
        scratch_shapes=[
            pltpu.VMEM((rows, static_width), jnp.bfloat16),
            pltpu.VMEM((rows, tv_width), jnp.bfloat16),
            pltpu.VMEM((2, BLOCK, BLOCK), jnp.float32),
            pltpu.VMEM((rows if rows > BLOCK else 8, static_width), jnp.float32),
            pltpu.VMEM((static_width, rows), jnp.bfloat16),
            pltpu.SemaphoreType.DMA((2,)),
            pltpu.SemaphoreType.DMA((n_col - 1,)),
            pltpu.SemaphoreType.DMA((n_col - 1,)),
            pltpu.SemaphoreType.DMA((2, n_row // 2, pieces)),
            pltpu.SemaphoreType.DMA((n_row // 2, pieces)),
            pltpu.SemaphoreType.DMA((n_row, pieces)),
        ],
        compiler_params=pltpu.CompilerParams(
            collective_id=0, has_side_effects=True, vmem_limit_bytes=40 * 1024 * 1024),
        cost_estimate=pl.CostEstimate(
            flops=2 * static_width * rows * tv_width, bytes_accessed=4 * static_width * tv_width, transcendentals=0),
    )(taps, arc_id.reshape(rows // BLOCK, BLOCK), static_design, tv_design)


def solution(mesh):
    return jax.shard_map(
        functools.partial(body, n_row=mesh.shape["row"], n_col=mesh.shape["col"]),
        mesh=mesh,
        in_specs=(P("col", "row"), P("row", "col"), P(), P()),
        out_specs=P("row", "col"),
        check_vma=False,
    )
```

time: 78.7 us -> 23 us (0.29)
  other arithmetic: 41.4 us -> 0 us
  blocking collectives: 26.5 us -> 0 us
  Pallas kernels: 0 us -> 18.2 us
  matrix products: 4.99 us -> 0 us
    add x2 -> x0, other arithmetic: 40.3 us -> none  [the longest x1 22 us: decorrelate(): forward + taps[step] * jnp.where(same, shift_down(block, step, 0.0), 0.0)]
    all_gather x2 -> x0, blocking collectives: 26.5 us -> none  [the longest x1 16.7 us: body(): all_rows = lax.all_gather(tv_design, 'row', axis=0, tiled=True)]
    pallas_call x0 -> x1, Pallas kernels: none -> 18.2 us  [body(): pl.pallas_call(functools.partial(kernel, n_row, n_col, pieces), out_shape...]
    dot_general x1 -> x0, matrix products: 4.99 us -> none  [body(): lax.dot_general(whole_static, all_rows, contract, preferred_element_type=...]
    unnamed x0 -> x9, local copies, waits for them, and re-layouts: none -> 4.59 us
    slice x5 -> x0, local copies, waits for them, and re-layouts: 4.11 us -> none  [the longest x1 2.06 us: decorrelate(): taps[step] * jnp.where(same, shift_up(forward, step, 0.0), 0.0)]
where the time goes in v1:
time: 23 us; the launch traced here: 22.8 us
  Pallas kernels  18.2 us (79%)
  local copies, waits for them, and re-layouts  4.59 us (20%)
    pallas_call x1, Pallas kernels, body(): pl.pallas_call(functools.partial(kernel, n_row, n_col, pieces), out_shape...  18.2 us
    unnamed x9, local copies, waits for them, and re-layouts  4.59 us

profile of v1, /device:TPU:0, one launch (start us, length us, event | category | flops | bytes accessed | tf_op | source)
XLA Modules:
  0.0 22.8 jit_solution(194658418937777672)
XLA Ops:
  0.0 0.0 copy-start
  0.0 0.9 %copy-done = bf16[16,3072]{1,0:T(8,128)(2,1)S(1)} copy-done((bf16[16,3072]{1,0:T(8,128)(2,1)S(1)}, bf16[16,3072]{1,0:T(8,128)(2,1)}, u32[]{:S(2)}) %copy-start) | copy-done | bytes 98328
  0.9 0.0 copy-start.1
  0.9 0.7 %copy-done.1 = bf16[32,256]{1,0:T(8,128)(2,1)S(1)} copy-done((bf16[32,256]{1,0:T(8,128)(2,1)S(1)}, bf16[32,256]{1,0:T(8,128)(2,1)}, u32[]{:S(2)}) %copy-start.1) | copy-done | bytes 16408
  1.6 0.0 copy-start.2
  1.6 0.7 %copy-done.2 = f32[32]{0:T(128)S(1)} copy-done((f32[32]{0:T(128)S(1)}, f32[32]{0:T(128)}, u32[]{:S(2)}) %copy-start.2) | copy-done | bytes 152
  2.3 0.0 copy-start.3
  2.3 0.7 %copy-done.3 = s32[128]{0:T(128)S(1)} copy-done((s32[128]{0:T(128)S(1)}, s32[128]{0:T(128)}, u32[]{:S(2)}) %copy-start.3) | copy-done | bytes 536
  2.9 18.2 %shard_map.46 = f32[256,3072]{1,0:T(8,128)S(1)} custom-call(f32[32]{0:T(128)S(1)} %copy-done.2, s32[1,128]{1,0:T(1,128)S(1)} %bitcast.1, bf16[32,256]{1,0:T(8,128)(2,1)S(1)} %copy-done.1, bf16[16,3072]{1,0:T(8,128)(2,1)S(1)} %copy-done), custom_call_target="tpu_custom_call" | custom-call | flops 201326592 | bytes 3145728 | tf_op jit(solution)/shard_map/pallas_call | solution.py:258
  21.1 1.7 %copy.6 = f32[256,3072]{1,0:T(8,128)} copy(f32[256,3072]{1,0:T(8,128)S(1)} %shard_map.46) | data formatting | bytes 6291456
Async XLA Ops:
  0.0 0.9 %copy-start = (bf16[16,3072]{1,0:T(8,128)(2,1)S(1)}, bf16[16,3072]{1,0:T(8,128)(2,1)}, u32[]{:S(2)}) copy-start(bf16[16,3072]{1,0:T(8,128)(2,1)} %tv_ref.1) | copy-start | bytes 294916
  0.9 0.7 %copy-start.1 = (bf16[32,256]{1,0:T(8,128)(2,1)S(1)}, bf16[32,256]{1,0:T(8,128)(2,1)}, u32[]{:S(2)}) copy-start(bf16[32,256]{1,0:T(8,128)(2,1)} %static_ref.1) | copy-start | bytes 49156
  1.6 0.7 %copy-start.2 = (f32[32]{0:T(128)S(1)}, f32[32]{0:T(128)}, u32[]{:S(2)}) copy-start(f32[32]{0:T(128)} %taps_ref.1) | copy-start | bytes 388
  2.3 0.7 %copy-start.3 = (s32[128]{0:T(128)S(1)}, s32[128]{0:T(128)}, u32[]{:S(2)}) copy-start(s32[128]{0:T(128)} %param.7) | copy-start | bytes 1540

commit v2 on v1

--- a/solution.py
+++ b/solution.py
@@ -12,9 +12,9 @@
 EXACT = lax.Precision.HIGHEST
 
 
-def toeplitz(taps_ref, offset):
+def toeplitz(taps_ref, offset, turned=False):
     shape = (BLOCK, BLOCK)
-    lag = lax.broadcasted_iota(jnp.int32, shape, 0) - lax.broadcasted_iota(jnp.int32, shape, 1) + offset
+    lag = lax.broadcasted_iota(jnp.int32, shape, int(turned)) - lax.broadcasted_iota(jnp.int32, shape, 1 - turned) + offset
     values = jnp.zeros(shape, jnp.float32)
     for step in range(taps_ref.shape[0]):
         values = jnp.where(lag == step, taps_ref[step], values)
@@ -36,8 +36,8 @@
 
 
 def kernel(
-    n_row, n_col, pieces, taps_ref, arc_ref, static_ref, tv_ref, out_ref,
-    static_all, tv_all, filter_ref, filtered_ref, weighted_ref,
+    n_row, n_col, pieces, taps_hbm, arc_hbm, static_ref, tv_ref, out_ref,
+    taps_ref, arc_ref, static_all, tv_all, filter_ref, filtered_ref, weighted_ref,
     own_sem, static_send, static_recv, line_send, pair_send, tv_recv,
 ):
     row, col = lax.axis_index("row"), lax.axis_index("col")
@@ -79,12 +79,22 @@
     own_static = pltpu.make_async_copy(static_ref, static_rows_of(col), own_sem.at[0])
     own_tv = pltpu.make_async_copy(
         tv_ref, tv_all.at[pl.ds(pl.multiple_of(row * tv_rows, tv_rows), tv_rows), :], own_sem.at[1])
+    own_taps = pltpu.make_async_copy(taps_hbm, taps_ref, own_sem.at[2])
+    own_arcs = pltpu.make_async_copy(arc_hbm, arc_ref, own_sem.at[3])
+    own_taps.start()
+    own_arcs.start()
     own_static.start()
     own_tv.start()
 
-    filter_ref[0] = toeplitz(taps_ref, 0)
+    own_taps.wait()
+    own_arcs.wait()
     if arc_ref.shape[0] > 1:
+        filter_ref[0] = toeplitz(taps_ref, 0)
         filter_ref[1] = toeplitz(taps_ref, BLOCK)
+    else:
+        same = same_arc(arc_ref[...], arc_ref[...])
+        filter_ref[0] = jnp.where(same, toeplitz(taps_ref, 0), 0.0)
+        filter_ref[1] = jnp.where(same, toeplitz(taps_ref, 0, True), 0.0)
 
     pl.semaphore_wait(barrier, n_col + has_up.astype(jnp.int32) + has_down.astype(jnp.int32))
 
@@ -105,15 +115,6 @@
             src_ref=window(chip_at, core_at, piece), dst_ref=window(chip_at, core_at, piece),
             send_sem=pair_send.at[chip_at, piece], recv_sem=tv_recv.at[chip_at * 2 + core_at, piece],
             device_id=at_row(chip, 1 - core), device_id_type=MESH)
-
-    for piece in range(pieces):
-        @pl.when(has_up)
-        def _():
-            to_line(own_window(piece), chip, piece, 0).start()
-
-        @pl.when(has_down)
-        def _():
-            to_line(own_window(piece), chip, piece, 1).start()
 
     def to_col(step):
         peer = (col + step) % n_col
@@ -124,6 +125,15 @@
 
     for step in range(1, n_col):
         to_col(step).start()
+    for piece in range(pieces):
+        @pl.when(has_up)
+        def _():
+            to_line(own_window(piece), chip, piece, 0).start()
+
+        @pl.when(has_down)
+        def _():
+            to_line(own_window(piece), chip, piece, 1).start()
+
     for piece in range(pieces):
         to_pair(own_window(piece), chip, piece).start()
 
@@ -161,12 +171,9 @@
         blocks = arc_ref.shape[0]
         contract = (((0,), (0,)), ((), ()))
         if blocks == 1:
-            arcs = arc_ref[...]
-            matrix = jnp.where(same_arc(arcs, arcs), filter_ref[0], 0.0)
-            filtered = jnp.dot(matrix, static_all[...].astype(jnp.float32),
-                               precision=EXACT, preferred_element_type=jnp.float32)
-            weighted = lax.dot_general(filtered, matrix, contract,
+            filtered = lax.dot_general(static_all[...].astype(jnp.float32), filter_ref[1], contract,
                                        precision=EXACT, preferred_element_type=jnp.float32)
+            weighted = jnp.dot(filtered, filter_ref[0], precision=EXACT, preferred_element_type=jnp.float32)
             weighted_ref[...] = weighted.astype(jnp.bfloat16)
             return
 
@@ -217,13 +224,13 @@
 
     for piece in range(pieces):
         forward(1, piece)
-    weigh()
 
     def middle(at):
         for piece in range(pieces):
             forward(at + 2, piece)
 
     along(chips - 3, middle, small)
+    weigh()
     for piece in range(pieces):
         forward(chips - 1, piece)
         if piece > 0:
@@ -253,20 +260,23 @@
     tv_rows, tv_width = tv_design.shape
     rows = tv_rows * n_row
     pieces = 4 if n_row <= 8 else 1
-    any_space = pl.BlockSpec(memory_space=pl.ANY)
+    hbm = pl.BlockSpec(memory_space=pltpu.HBM)
+    operands = (taps, arc_id.reshape(rows // BLOCK, BLOCK), static_design, tv_design)
     vmem = pl.BlockSpec(memory_space=pltpu.VMEM)
     return pl.pallas_call(
         functools.partial(kernel, n_row, n_col, pieces),
         out_shape=jax.ShapeDtypeStruct((static_width, tv_width), jnp.float32),
-        in_specs=[pl.BlockSpec(memory_space=pltpu.SMEM), vmem, any_space, any_space],
+        in_specs=[hbm, hbm, hbm, hbm],
         out_specs=vmem,
         scratch_shapes=[
+            pltpu.SMEM(taps.shape, jnp.float32),
+            pltpu.VMEM((rows // BLOCK, BLOCK), jnp.int32),
             pltpu.VMEM((rows, static_width), jnp.bfloat16),
             pltpu.VMEM((rows, tv_width), jnp.bfloat16),
             pltpu.VMEM((2, BLOCK, BLOCK), jnp.float32),
             pltpu.VMEM((rows if rows > BLOCK else 8, static_width), jnp.float32),
             pltpu.VMEM((static_width, rows), jnp.bfloat16),
-            pltpu.SemaphoreType.DMA((2,)),
+            pltpu.SemaphoreType.DMA((4,)),
             pltpu.SemaphoreType.DMA((n_col - 1,)),
             pltpu.SemaphoreType.DMA((n_col - 1,)),
             pltpu.SemaphoreType.DMA((2, n_row // 2, pieces)),
@@ -277,7 +287,7 @@
             collective_id=0, has_side_effects=True, vmem_limit_bytes=40 * 1024 * 1024),
         cost_estimate=pl.CostEstimate(
             flops=2 * static_width * rows * tv_width, bytes_accessed=4 * static_width * tv_width, transcendentals=0),
-    )(taps, arc_id.reshape(rows // BLOCK, BLOCK), static_design, tv_design)
+    )(*(pltpu.with_memory_space_constraint(value, pltpu.HBM) for value in operands))
 
 
 def solution(mesh):

time: 23 us -> 19.7 us (0.86)
  local copies, waits for them, and re-layouts: 4.59 us -> 1.67 us
  Pallas kernels: 18.2 us -> 17.9 us
    unnamed x9 -> x1, local copies, waits for them, and re-layouts: 4.59 us -> 1.67 us
    pallas_call x1, Pallas kernels: 18.2 us -> 17.9 us  [body(): pl.pallas_call(functools.partial(kernel, n_row, n_col, pieces), out_shape...]
where the time goes in v2:
time: 19.7 us; the launch traced here: 19.5 us
  Pallas kernels  17.9 us (91%)
  local copies, waits for them, and re-layouts  1.67 us (8%)
    pallas_call x1, Pallas kernels, body(): pl.pallas_call(functools.partial(kernel, n_row, n_col, pieces), out_shape...  17.9 us
    unnamed x1, local copies, waits for them, and re-layouts  1.67 us

profile of v2, /device:TPU:0, one launch (start us, length us, event | category | flops | bytes accessed | tf_op | source)
XLA Modules:
  0.0 19.5 jit_solution(3795463193552652547)
XLA Ops:
  0.0 17.9 %shard_map.46 = f32[256,3072]{1,0:T(8,128)S(1)} custom-call(f32[32]{0:T(128)} %taps_hbm.1, s32[1,128]{1,0:T(1,128)} %bitcast.1, bf16[32,256]{1,0:T(8,128)(2,1)} %static_ref.1, bf16[16,3072]{1,0:T(8,128)(2,1)} %tv_ref.1), custom_call_target="tpu_custom_call" | custom-call | flops 201326592 | bytes 3145728 | tf_op jit(solution)/shard_map/pallas_call | solution.py:266
  17.9 1.7 %copy.6 = f32[256,3072]{1,0:T(8,128)} copy(f32[256,3072]{1,0:T(8,128)S(1)} %shard_map.46) | data formatting | bytes 6291456

commit v3 on v2

--- a/solution.py
+++ b/solution.py
@@ -50,20 +50,14 @@
     def at_row(chip_at, core_at):
         return (chip_at * 2 + core_at, col)
 
-    has_up, has_down = chip < chips - 1, chip > 0
 
     barrier = pltpu.get_barrier_semaphore()
     for step in range(1, n_col):
         pl.semaphore_signal(barrier, inc=1, device_id=(row, (col + step) % n_col), device_id_type=MESH)
     pl.semaphore_signal(barrier, inc=1, device_id=at_row(chip, 1 - core), device_id_type=MESH)
 
-    @pl.when(has_up)
-    def _():
-        pl.semaphore_signal(barrier, inc=1, device_id=at_row(chip + 1, core), device_id_type=MESH)
-
-    @pl.when(has_down)
-    def _():
-        pl.semaphore_signal(barrier, inc=1, device_id=at_row(chip - 1, core), device_id_type=MESH)
+    along(chips - 1, lambda at: pl.semaphore_signal(
+        barrier, inc=1, device_id=at_row((chip + at + 1) % chips, core), device_id_type=MESH), small)
 
     def static_rows_of(at):
         return static_all.at[pl.ds(pl.multiple_of(at * static_rows, static_rows), static_rows), :]
@@ -86,6 +80,59 @@
     own_static.start()
     own_tv.start()
 
+    pl.semaphore_wait(barrier, n_col + chips - 1)
+
+    def to_line(src, chip_at, piece, way):
+        return pltpu.make_async_remote_copy(
+            src_ref=src, dst_ref=window(chip_at, core, piece),
+            send_sem=line_send.at[way, chip_at, piece], recv_sem=tv_recv.at[chip_at * 2 + core, piece],
+            device_id=at_row(chip + 1 - 2 * way, core), device_id_type=MESH)
+
+    def to_pair(src, chip_at, piece):
+        return pltpu.make_async_remote_copy(
+            src_ref=src, dst_ref=window(chip_at, core, piece),
+            send_sem=pair_send.at[chip_at, piece], recv_sem=tv_recv.at[chip_at * 2 + core, piece],
+            device_id=at_row(chip, 1 - core), device_id_type=MESH)
+
+    def arrival(chip_at, core_at, piece):
+        return pltpu.make_async_remote_copy(
+            src_ref=window(chip_at, core_at, piece), dst_ref=window(chip_at, core_at, piece),
+            send_sem=pair_send.at[chip_at, piece], recv_sem=tv_recv.at[chip_at * 2 + core_at, piece],
+            device_id=at_row(chip, 1 - core), device_id_type=MESH)
+
+    def to_col(step):
+        peer = (col + step) % n_col
+        return pltpu.make_async_remote_copy(
+            src_ref=static_ref, dst_ref=static_rows_of(col),
+            send_sem=static_send.at[step - 1], recv_sem=static_recv.at[step - 1],
+            device_id=(row, peer), device_id_type=MESH)
+
+    for step in range(1, n_col):
+        to_col(step).start()
+    def to_chip(target, piece):
+        return pltpu.make_async_remote_copy(
+            src_ref=own_window(piece), dst_ref=window(chip, core, piece),
+            send_sem=line_send.at[2, target, piece], recv_sem=tv_recv.at[chip * 2 + core, piece],
+            device_id=at_row(target, core), device_id_type=MESH)
+
+    def pushes(target):
+        inside = jnp.logical_and(target >= 0, jnp.logical_and(target < chips, target != chip))
+        low = jnp.logical_and(target == 0, chip == 2)
+        high = jnp.logical_and(target == chips - 1, chip == chips - 3)
+        return jnp.logical_and(inside, jnp.logical_not(jnp.logical_or(low, high)))
+
+    def push(at):
+        distance = at + 1
+        for target in (chip - distance, chip + distance):
+            @pl.when(pushes(target))
+            def _():
+                for piece in range(pieces):
+                    to_chip(target, piece).start()
+
+    along(chips - 1, push, small)
+    for piece in range(pieces):
+        to_pair(own_window(piece), chip, piece).start()
+
     own_taps.wait()
     own_arcs.wait()
     if arc_ref.shape[0] > 1:
@@ -96,47 +143,6 @@
         filter_ref[0] = jnp.where(same, toeplitz(taps_ref, 0), 0.0)
         filter_ref[1] = jnp.where(same, toeplitz(taps_ref, 0, True), 0.0)
 
-    pl.semaphore_wait(barrier, n_col + has_up.astype(jnp.int32) + has_down.astype(jnp.int32))
-
-    def to_line(src, chip_at, piece, way):
-        return pltpu.make_async_remote_copy(
-            src_ref=src, dst_ref=window(chip_at, core, piece),
-            send_sem=line_send.at[way, chip_at, piece], recv_sem=tv_recv.at[chip_at * 2 + core, piece],
-            device_id=at_row(chip + 1 - 2 * way, core), device_id_type=MESH)
-
-    def to_pair(src, chip_at, piece):
-        return pltpu.make_async_remote_copy(
-            src_ref=src, dst_ref=window(chip_at, core, piece),
-            send_sem=pair_send.at[chip_at, piece], recv_sem=tv_recv.at[chip_at * 2 + core, piece],
-            device_id=at_row(chip, 1 - core), device_id_type=MESH)
-
-    def arrival(chip_at, core_at, piece):
-        return pltpu.make_async_remote_copy(
-            src_ref=window(chip_at, core_at, piece), dst_ref=window(chip_at, core_at, piece),
-            send_sem=pair_send.at[chip_at, piece], recv_sem=tv_recv.at[chip_at * 2 + core_at, piece],
-            device_id=at_row(chip, 1 - core), device_id_type=MESH)
-
-    def to_col(step):
-        peer = (col + step) % n_col
-        return pltpu.make_async_remote_copy(
-            src_ref=static_ref, dst_ref=static_rows_of(col),
-            send_sem=static_send.at[step - 1], recv_sem=static_recv.at[step - 1],
-            device_id=(row, peer), device_id_type=MESH)
-
-    for step in range(1, n_col):
-        to_col(step).start()
-    for piece in range(pieces):
-        @pl.when(has_up)
-        def _():
-            to_line(own_window(piece), chip, piece, 0).start()
-
-        @pl.when(has_down)
-        def _():
-            to_line(own_window(piece), chip, piece, 1).start()
-
-    for piece in range(pieces):
-        to_pair(own_window(piece), chip, piece).start()
-
     def forward(hop, piece):
         below, above = chip - hop, chip + hop
 
@@ -144,7 +150,7 @@
         def _():
             arrival(below, core, piece).wait_recv()
 
-            @pl.when(has_up)
+            @pl.when(jnp.logical_and(chip == chips - 2, hop == 1))
             def _():
                 to_line(window(below, core, piece), below, piece, 0).start()
 
@@ -154,7 +160,7 @@
         def _():
             arrival(above, core, piece).wait_recv()
 
-            @pl.when(has_down)
+            @pl.when(jnp.logical_and(chip == 1, hop == 1))
             def _():
                 to_line(window(above, core, piece), above, piece, 1).start()
 
@@ -242,24 +248,28 @@
 
     def sent(chip_at):
         for piece in range(pieces):
-            @pl.when(jnp.logical_and(has_up, chip_at <= chip))
+            @pl.when(pushes(chip_at))
             def _():
-                to_line(own_window(piece), chip_at, piece, 0).wait_send()
-
-            @pl.when(jnp.logical_and(has_down, chip_at >= chip))
-            def _():
-                to_line(own_window(piece), chip_at, piece, 1).wait_send()
+                to_chip(chip_at, piece).wait_send()
 
             to_pair(own_window(piece), chip_at, piece).wait_send()
 
     along(chips, sent, small)
+    for piece in range(pieces):
+        @pl.when(chip == 1)
+        def _():
+            to_line(own_window(piece), 2, piece, 1).wait_send()
+
+        @pl.when(chip == chips - 2)
+        def _():
+            to_line(own_window(piece), chips - 3, piece, 0).wait_send()
 
 
 def body(static_design, tv_design, taps, arc_id, n_row, n_col):
     static_rows, static_width = static_design.shape
     tv_rows, tv_width = tv_design.shape
     rows = tv_rows * n_row
-    pieces = 4 if n_row <= 8 else 1
+    pieces = 2 if n_row <= 8 else 1
     hbm = pl.BlockSpec(memory_space=pltpu.HBM)
     operands = (taps, arc_id.reshape(rows // BLOCK, BLOCK), static_design, tv_design)
     vmem = pl.BlockSpec(memory_space=pltpu.VMEM)
@@ -279,7 +289,7 @@
             pltpu.SemaphoreType.DMA((4,)),
             pltpu.SemaphoreType.DMA((n_col - 1,)),
             pltpu.SemaphoreType.DMA((n_col - 1,)),
-            pltpu.SemaphoreType.DMA((2, n_row // 2, pieces)),
+            pltpu.SemaphoreType.DMA((3, n_row // 2, pieces)),
             pltpu.SemaphoreType.DMA((n_row // 2, pieces)),
             pltpu.SemaphoreType.DMA((n_row, pieces)),
         ],

time: 19.7 us -> 18 us (0.914)
  the two profiles are of different devices: /device:TPU:0 before, /device:TPU:1 now
where the time goes in v3:
time: 18 us; the launch traced here: 17.8 us
  Pallas kernels  16.2 us (90%)
  local copies, waits for them, and re-layouts  1.67 us (9%)
    pallas_call x1, Pallas kernels, body(): pl.pallas_call(functools.partial(kernel, n_row, n_col, pieces), out_shape...  16.2 us
    unnamed x1, local copies, waits for them, and re-layouts  1.67 us

profile of v3, /device:TPU:1, one launch (start us, length us, event | category | flops | bytes accessed | tf_op | source)
XLA Modules:
  0.0 17.8 jit_solution(8352838206528829476)
XLA Ops:
  0.0 16.2 %shard_map.46 = f32[256,3072]{1,0:T(8,128)S(1)} custom-call(f32[32]{0:T(128)} %taps_hbm.1, s32[1,128]{1,0:T(1,128)} %bitcast.1, bf16[32,256]{1,0:T(8,128)(2,1)} %static_ref.1, bf16[16,3072]{1,0:T(8,128)(2,1)} %tv_ref.1), custom_call_target="tpu_custom_call" | custom-call | flops 201326592 | bytes 3145728 | tf_op jit(solution)/shard_map/pallas_call | solution.py:276
  16.2 1.7 %copy.6 = f32[256,3072]{1,0:T(8,128)} copy(f32[256,3072]{1,0:T(8,128)S(1)} %shard_map.46) | data formatting | bytes 6291456

commit v4 on v3

--- a/solution.py
+++ b/solution.py
@@ -36,8 +36,8 @@
 
 
 def kernel(
-    n_row, n_col, pieces, taps_hbm, arc_hbm, static_ref, tv_ref, out_ref,
-    taps_ref, arc_ref, static_all, tv_all, filter_ref, filtered_ref, weighted_ref,
+    n_row, n_col, pieces, taps_hbm, arc_hbm, static_ref, tv_ref, weighted_ref, tv_all,
+    taps_ref, arc_ref, static_all, filter_ref, filtered_ref,
     own_sem, static_send, static_recv, line_send, pair_send, tv_recv,
 ):
     row, col = lax.axis_index("row"), lax.axis_index("col")
@@ -107,8 +107,6 @@
             send_sem=static_send.at[step - 1], recv_sem=static_recv.at[step - 1],
             device_id=(row, peer), device_id_type=MESH)
 
-    for step in range(1, n_col):
-        to_col(step).start()
     def to_chip(target, piece):
         return pltpu.make_async_remote_copy(
             src_ref=own_window(piece), dst_ref=window(chip, core, piece),
@@ -129,19 +127,15 @@
                 for piece in range(pieces):
                     to_chip(target, piece).start()
 
-    along(chips - 1, push, small)
+    push(0)
+
     for piece in range(pieces):
         to_pair(own_window(piece), chip, piece).start()
 
-    own_taps.wait()
-    own_arcs.wait()
-    if arc_ref.shape[0] > 1:
-        filter_ref[0] = toeplitz(taps_ref, 0)
-        filter_ref[1] = toeplitz(taps_ref, BLOCK)
-    else:
-        same = same_arc(arc_ref[...], arc_ref[...])
-        filter_ref[0] = jnp.where(same, toeplitz(taps_ref, 0), 0.0)
-        filter_ref[1] = jnp.where(same, toeplitz(taps_ref, 0, True), 0.0)
+    for step in range(1, n_col):
+        to_col(step).start()
+
+    along(chips - 2, lambda at: push(at + 1), small)
 
     def forward(hop, piece):
         below, above = chip - hop, chip + hop
@@ -224,12 +218,19 @@
         along(chips, paired, small)
         if piece == 0:
             own_tv.wait()
-        columns = pl.ds(piece * width, width)
-        out_ref[:, columns] = jnp.dot(
-            weighted_ref[...], tv_all[:, columns], preferred_element_type=jnp.float32)
 
     for piece in range(pieces):
         forward(1, piece)
+
+    own_taps.wait()
+    own_arcs.wait()
+    if arc_ref.shape[0] > 1:
+        filter_ref[0] = toeplitz(taps_ref, 0)
+        filter_ref[1] = toeplitz(taps_ref, BLOCK)
+    else:
+        same = same_arc(arc_ref[...], arc_ref[...])
+        filter_ref[0] = jnp.where(same, toeplitz(taps_ref, 0), 0.0)
+        filter_ref[1] = jnp.where(same, toeplitz(taps_ref, 0, True), 0.0)
 
     def middle(at):
         for piece in range(pieces):
@@ -263,6 +264,18 @@
         @pl.when(chip == chips - 2)
         def _():
             to_line(own_window(piece), chips - 3, piece, 0).wait_send()
+
+
+def multiply_out(pieces, weighted_ref, tv_ref, out_ref, held, sems):
+    width = tv_ref.shape[1] // pieces
+    copies = []
+    for piece in range(pieces):
+        columns = pl.ds(piece * width, width)
+        held[:, columns] = jnp.dot(weighted_ref[...], tv_ref[:, columns], preferred_element_type=jnp.float32)
+        copies.append(pltpu.make_async_copy(held.at[:, columns], out_ref.at[:, columns], sems.at[piece]))
+        copies[-1].start()
+    for copy in copies:
+        copy.wait()
 
 
 def body(static_design, tv_design, taps, arc_id, n_row, n_col):
@@ -273,19 +286,17 @@
     hbm = pl.BlockSpec(memory_space=pltpu.HBM)
     operands = (taps, arc_id.reshape(rows // BLOCK, BLOCK), static_design, tv_design)
     vmem = pl.BlockSpec(memory_space=pltpu.VMEM)
-    return pl.pallas_call(
+    weighted, gathered = pl.pallas_call(
         functools.partial(kernel, n_row, n_col, pieces),
-        out_shape=jax.ShapeDtypeStruct((static_width, tv_width), jnp.float32),
+        out_shape=(jax.ShapeDtypeStruct((static_width, rows), jnp.bfloat16), jax.ShapeDtypeStruct((rows, tv_width), jnp.bfloat16)),
         in_specs=[hbm, hbm, hbm, hbm],
-        out_specs=vmem,
+        out_specs=(vmem, vmem),
         scratch_shapes=[
             pltpu.SMEM(taps.shape, jnp.float32),
             pltpu.VMEM((rows // BLOCK, BLOCK), jnp.int32),
             pltpu.VMEM((rows, static_width), jnp.bfloat16),
-            pltpu.VMEM((rows, tv_width), jnp.bfloat16),
             pltpu.VMEM((2, BLOCK, BLOCK), jnp.float32),
             pltpu.VMEM((rows if rows > BLOCK else 8, static_width), jnp.float32),
-            pltpu.VMEM((static_width, rows), jnp.bfloat16),
             pltpu.SemaphoreType.DMA((4,)),
             pltpu.SemaphoreType.DMA((n_col - 1,)),
             pltpu.SemaphoreType.DMA((n_col - 1,)),
@@ -298,6 +309,18 @@
         cost_estimate=pl.CostEstimate(
             flops=2 * static_width * rows * tv_width, bytes_accessed=4 * static_width * tv_width, transcendentals=0),
     )(*(pltpu.with_memory_space_constraint(value, pltpu.HBM) for value in operands))
+    parts = 6
+    return pl.pallas_call(
+        functools.partial(multiply_out, parts),
+        out_shape=jax.ShapeDtypeStruct((static_width, tv_width), jnp.float32),
+        in_specs=[vmem, vmem],
+        out_specs=pl.BlockSpec(memory_space=pltpu.HBM),
+        scratch_shapes=[
+            pltpu.VMEM((static_width, tv_width), jnp.float32),
+            pltpu.SemaphoreType.DMA((parts,)),
+        ],
+        compiler_params=pltpu.CompilerParams(vmem_limit_bytes=32 * 1024 * 1024),
+    )(weighted, gathered)
 
 
 def solution(mesh):

time: 18 us -> 17.9 us (level)
  the two profiles are of different devices: /device:TPU:1 before, /device:TPU:0 now
where the time goes in v4:
time: 17.9 us; the launch traced here: 17.8 us
  Pallas kernels  17.8 us (99%)
    pallas_call x1, Pallas kernels, body(): pl.pallas_call(functools.partial(kernel, n_row, n_col, pieces), out_shape...  15.9 us
    pallas_call x1, Pallas kernels, body(): pl.pallas_call(functools.partial(multiply_out, parts), out_shape=jax.Shap...  1.92 us

profile of v4, /device:TPU:0, one launch (start us, length us, event | category | flops | bytes accessed | tf_op | source)
XLA Modules:
  0.0 17.8 jit_solution(9468352048651728651)
XLA Ops:
  0.0 15.9 %shard_map.46 = (bf16[256,128]{1,0:T(8,128)(2,1)S(1)}, bf16[128,3072]{1,0:T(8,128)(2,1)S(1)}) custom-call(f32[32]{0:T(128)} %taps_hbm.1, s32[1,128]{1,0:T(1,128)} %bitcast.1, bf16[32,256]{1,0:T(8,128)(2,1)} %static_ref.1, bf16[16,3072]{1,0:T(8,128)(2,1)} %tv_ref.1), custom_call_target="tpu_custom_call" | custom-call | flops 201326592 | bytes 3145728 | tf_op jit(solution)/shard_map/pallas_call | solution.py:289
  15.9 1.9 %shard_map.47 = f32[256,3072]{1,0:T(8,128)} custom-call(bf16[256,128]{1,0:T(8,128)(2,1)S(1)} %get-tuple-element.7.weighted_ref, bf16[128,3072]{1,0:T(8,128)(2,1)S(1)} %get-tuple-element.8.tv_ref), custom_call_target="tpu_custom_call" | custom-call | tf_op jit(solution)/shard_map/pallas_call | solution.py:313
